TPU v7x, 256 devices: a whole 4x4x8 slice. The times are simulated.
256 devices in a mesh: row: 16 (over x_lo, z), col: 16 (over x_hi, y, core).
Axes of the slice: x: 4 (x_hi: 2, x_lo: 2; x = x_hi * 2 + x_lo), y: 4, z: 8, core: 2. Of those that a mesh axis runs over, the one named last changes fastest.
Arguments:
- queries: bfloat16 [192, 512, 2048], P('row', 'col'), may hold values from -192 to 192
- key_vectors: bfloat16 [192, 512, 2048], P('row', 'col'), may hold values from -6 to 6
- value_vectors: bfloat16 [192, 512, 2048], P('row', 'col'), may hold values from -6 to 6
- grad_output: bfloat16 [192, 512, 2048], P('row', 'col'), may hold values from -6 to 6
Outputs:
- grad_queries: bfloat16 [192, 512, 2048], P('row', 'col')
- grad_keys: bfloat16 [192, 512, 2048], P('row', 'col')
- grad_values: bfloat16 [192, 512, 2048], P('row', 'col')
All inputs are finite; a program needn't handle non-finite values.
Results may differ from a plain program's by a relative error of at most 0.012.
The roundings to bfloat16 on the way count: a program that leaves them out, or rounds other values in their place, can miss the bound.
Values may be sent and summed in bfloat16 or wider, within the bound.
A program may use at most 128 MiB of HBM per device.

v0:
```python
import math

import jax
import jax.numpy as jnp
from jax import lax
from jax.sharding import PartitionSpec as P

HEAD_DIM = 128


def attend_back(query_block, key_block, value_block, grad_block):
    length = query_block.shape[1]
    factor = 1.0 / math.sqrt(query_block.shape[2])
    scores = (
        jnp.einsum("gqe,gke->gqk", query_block, key_block, preferred_element_type=jnp.float32)
        * factor
    )
    position = lax.broadcasted_iota(jnp.int32, (length, length), 0)
    column_index = lax.broadcasted_iota(jnp.int32, (length, length), 1)
    scores = jnp.where(column_index <= position, scores, -jnp.inf)
    highest = jnp.max(scores, axis=-1, keepdims=True)
    weights = jnp.exp(scores - highest)
    probability = weights / jnp.sum(weights, axis=-1, keepdims=True)
    weights_low = probability.astype(jnp.bfloat16)
    attended = jnp.einsum(
        "gqk,gke->gqe", weights_low, value_block, preferred_element_type=jnp.float32
    )
    correction = jnp.sum(grad_block.astype(jnp.float32) * attended, axis=-1, keepdims=True)
    grad_weights = jnp.einsum(
        "gqe,gke->gqk", grad_block, value_block, preferred_element_type=jnp.float32
    )
    grad_scores = (probability * (grad_weights - correction)).astype(jnp.bfloat16)
    grad_value = jnp.einsum(
        "gqk,gqe->gke", weights_low, grad_block, preferred_element_type=jnp.float32
    )
    grad_query = (
        jnp.einsum("gqk,gke->gqe", grad_scores, key_block, preferred_element_type=jnp.float32)
        * factor
    )
    grad_key = (
        jnp.einsum("gqk,gqe->gke", grad_scores, query_block, preferred_element_type=jnp.float32)
        * factor
    )
    return (
        grad_query.astype(jnp.bfloat16),
        grad_key.astype(jnp.bfloat16),
        grad_value.astype(jnp.bfloat16),
    )


def item_block(pieces):
    outcome = attend_back(pieces[0][0], pieces[1][0], pieces[2][0], pieces[3][0])
    return (outcome[0][None], outcome[1][None], outcome[2][None])


def body(queries, key_vectors, value_vectors, grad_output):
    row_count, col_count, width = queries.shape
    half_width = width // 2
    heads_half = half_width // HEAD_DIM
    col_devices = lax.axis_size("col")
    row_devices = lax.axis_size("row")
    row_groups = row_count * heads_half // col_devices
    col_groups = col_count * heads_half // row_devices

    def row_items(array):
        local = array[:, :, :half_width].reshape(row_count, col_count, heads_half, HEAD_DIM)
        return local.transpose(0, 2, 1, 3).reshape(col_devices, row_groups, col_count, HEAD_DIM)

    def col_items(array):
        local = array[:, :, half_width:].reshape(row_count, col_count, heads_half, HEAD_DIM)
        return local.transpose(1, 2, 0, 3).reshape(row_devices, col_groups, row_count, HEAD_DIM)

    def row_layout(array):
        shaped = array.reshape(row_count, heads_half, col_count, HEAD_DIM)
        return shaped.transpose(0, 2, 1, 3).reshape(row_count, col_count, half_width)

    def col_layout(array):
        shaped = array.reshape(col_count, heads_half, row_count, HEAD_DIM)
        return shaped.transpose(2, 0, 1, 3).reshape(row_count, col_count, half_width)

    row_query = row_items(queries)
    row_key = row_items(key_vectors)
    row_value = row_items(value_vectors)
    row_grad = row_items(grad_output)
    col_query = col_items(queries)
    col_key = col_items(key_vectors)
    col_value = col_items(value_vectors)
    col_grad = col_items(grad_output)
    whole_rows = (
        lax.all_to_all(row_query, "col", split_axis=0, concat_axis=2, tiled=True),
        lax.all_to_all(row_key, "col", split_axis=0, concat_axis=2, tiled=True),
        lax.all_to_all(row_value, "col", split_axis=0, concat_axis=2, tiled=True),
        lax.all_to_all(row_grad, "col", split_axis=0, concat_axis=2, tiled=True),
    )
    row_results = item_block(whole_rows)
    whole_cols = (
        lax.all_to_all(col_query, "row", split_axis=0, concat_axis=2, tiled=True),
        lax.all_to_all(col_key, "row", split_axis=0, concat_axis=2, tiled=True),
        lax.all_to_all(col_value, "row", split_axis=0, concat_axis=2, tiled=True),
        lax.all_to_all(col_grad, "row", split_axis=0, concat_axis=2, tiled=True),
    )
    col_results = item_block(whole_cols)
    back_rows = (
        lax.all_to_all(row_results[0], "col", split_axis=2, concat_axis=0, tiled=True),
        lax.all_to_all(row_results[1], "col", split_axis=2, concat_axis=0, tiled=True),
        lax.all_to_all(row_results[2], "col", split_axis=2, concat_axis=0, tiled=True),
    )
    back_cols = (
        lax.all_to_all(col_results[0], "row", split_axis=2, concat_axis=0, tiled=True),
        lax.all_to_all(col_results[1], "row", split_axis=2, concat_axis=0, tiled=True),
        lax.all_to_all(col_results[2], "row", split_axis=2, concat_axis=0, tiled=True),
    )
    grad_queries = jnp.concatenate([row_layout(back_rows[0]), col_layout(back_cols[0])], axis=2)
    grad_keys = jnp.concatenate([row_layout(back_rows[1]), col_layout(back_cols[1])], axis=2)
    grad_values = jnp.concatenate([row_layout(back_rows[2]), col_layout(back_cols[2])], axis=2)
    return (grad_queries, grad_keys, grad_values)


def solution(mesh):
    placed = (
        P("row", "col", None),
        P("row", "col", None),
        P("row", "col", None),
        P("row", "col", None),
    )
    return jax.shard_map(
        body,
        mesh=mesh,
        in_specs=placed,
        out_specs=(P("row", "col", None), P("row", "col", None), P("row", "col", None)),
        check_vma=False,
    )
```

profile of v0, /device:TPU:4, one launch (start us, length us, event | category | flops | bytes accessed | tf_op | source)
XLA Modules:
  0.0 343.5 jit_solution(784496328378427418)
XLA Ops:
  4.4 7.5 %all-to-all-start = ((bf16[16,6,32,128]{3,2,1,0:T(8,128)(2,1)}), bf16[16,6,32,128]{3,2,1,0:T(8,128)(2,1)S(1)}, u32[]{:S(2)}, u32[]{:S(2)}) async-start(bf16[16,6,32,128]{3,2,1,0:T(8,128)(2,1)} %bitcast.1), calls=%async_computation | async-start | bytes 1572864 | tf_op jit(solution)/shard_map/all_to_all | solution.py:90
  14.1 10.1 %all-to-all-done = bf16[16,6,32,128]{3,2,1,0:T(8,128)(2,1)S(1)} async-done(((bf16[16,6,32,128]{3,2,1,0:T(8,128)(2,1)}), bf16[16,6,32,128]{3,2,1,0:T(8,128)(2,1)S(1)}, u32[]{:S(2)}, u32[]{:S(2)}) %all-to-all-start) | async-done | bytes 786464 | tf_op jit(solution)/shard_map/all_to_all | solution.py:90
  24.2 6.4 %all-to-all-start.1 = ((bf16[16,6,32,128]{3,2,1,0:T(8,128)(2,1)}), bf16[16,6,32,128]{3,2,1,0:T(8,128)(2,1)S(1)}, u32[]{:S(2)}, u32[]{:S(2)}) async-start(bf16[16,6,32,128]{3,2,1,0:T(8,128)(2,1)} %bitcast.6), calls=%async_computation.1 | async-start | bytes 1572864 | tf_op jit(solution)/shard_map/all_to_all | solution.py:91
  34.2 8.6 %all-to-all-done.1 = bf16[16,6,32,128]{3,2,1,0:T(8,128)(2,1)S(1)} async-done(((bf16[16,6,32,128]{3,2,1,0:T(8,128)(2,1)}), bf16[16,6,32,128]{3,2,1,0:T(8,128)(2,1)S(1)}, u32[]{:S(2)}, u32[]{:S(2)}) %all-to-all-start.1) | async-done | bytes 786464 | tf_op jit(solution)/shard_map/all_to_all | solution.py:91
  42.9 6.4 %all-to-all-start.3 = ((bf16[16,6,32,128]{3,2,1,0:T(8,128)(2,1)}), bf16[16,6,32,128]{3,2,1,0:T(8,128)(2,1)S(1)}, u32[]{:S(2)}, u32[]{:S(2)}) async-start(bf16[16,6,32,128]{3,2,1,0:T(8,128)(2,1)} %bitcast.16), calls=%async_computation.3 | async-start | bytes 1572864 | tf_op jit(solution)/shard_map/all_to_all | solution.py:92
  53.0 8.6 %all-to-all-done.3 = bf16[16,6,32,128]{3,2,1,0:T(8,128)(2,1)S(1)} async-done(((bf16[16,6,32,128]{3,2,1,0:T(8,128)(2,1)}), bf16[16,6,32,128]{3,2,1,0:T(8,128)(2,1)S(1)}, u32[]{:S(2)}, u32[]{:S(2)}) %all-to-all-start.3) | async-done | bytes 786464 | tf_op jit(solution)/shard_map/all_to_all | solution.py:92
  61.6 6.4 %all-to-all-start.2 = ((bf16[16,6,32,128]{3,2,1,0:T(8,128)(2,1)}), bf16[16,6,32,128]{3,2,1,0:T(8,128)(2,1)S(1)}, u32[]{:S(2)}, u32[]{:S(2)}) async-start(bf16[16,6,32,128]{3,2,1,0:T(8,128)(2,1)} %bitcast.202), calls=%async_computation.2 | async-start | bytes 1572864 | tf_op jit(solution)/shard_map/all_to_all | solution.py:93
  70.4 9.9 %all-to-all-done.2 = bf16[16,6,32,128]{3,2,1,0:T(8,128)(2,1)S(1)} async-done(((bf16[16,6,32,128]{3,2,1,0:T(8,128)(2,1)}), bf16[16,6,32,128]{3,2,1,0:T(8,128)(2,1)S(1)}, u32[]{:S(2)}, u32[]{:S(2)}) %all-to-all-start.2) | async-done | bytes 786464 | tf_op jit(solution)/shard_map/all_to_all | solution.py:93
  81.3 9.3 %all-to-all-start.5 = ((bf16[16,16,12,128]{3,1,2,0:T(8,128)(2,1)}), bf16[16,16,12,128]{3,1,2,0:T(8,128)(2,1)S(1)}, u32[]{:S(2)}, u32[]{:S(2)}) async-start(bf16[16,16,12,128]{3,1,2,0:T(8,128)(2,1)} %copy.148), calls=%async_computation.5 | async-start | bytes 1572864 | tf_op jit(solution)/shard_map/all_to_all | solution.py:97
  93.1 19.2 %all-to-all-done.5 = bf16[16,16,12,128]{3,1,2,0:T(8,128)(2,1)S(1)} async-done(((bf16[16,16,12,128]{3,1,2,0:T(8,128)(2,1)}), bf16[16,16,12,128]{3,1,2,0:T(8,128)(2,1)S(1)}, u32[]{:S(2)}, u32[]{:S(2)}) %all-to-all-start.5) | async-done | bytes 786464 | tf_op jit(solution)/shard_map/all_to_all | solution.py:97
  112.2 4.5 %all-to-all-start.6 = ((bf16[16,16,12,128]{3,1,2,0:T(8,128)(2,1)}), bf16[16,16,12,128]{3,1,2,0:T(8,128)(2,1)S(1)}, u32[]{:S(2)}, u32[]{:S(2)}) async-start(bf16[16,16,12,128]{3,1,2,0:T(8,128)(2,1)} %copy.149), calls=%async_computation.6 | async-start | bytes 1572864 | tf_op jit(solution)/shard_map/all_to_all | solution.py:98
  120.5 17.6 %all-to-all-done.6 = bf16[16,16,12,128]{3,1,2,0:T(8,128)(2,1)S(1)} async-done(((bf16[16,16,12,128]{3,1,2,0:T(8,128)(2,1)}), bf16[16,16,12,128]{3,1,2,0:T(8,128)(2,1)S(1)}, u32[]{:S(2)}, u32[]{:S(2)}) %all-to-all-start.6) | async-done | bytes 786464 | tf_op jit(solution)/shard_map/all_to_all | solution.py:98
  138.1 4.7 %all-to-all-start.8 = ((bf16[16,16,12,128]{3,1,2,0:T(8,128)(2,1)}), bf16[16,16,12,128]{3,1,2,0:T(8,128)(2,1)}, u32[]{:S(2)}, u32[]{:S(2)}) async-start(bf16[16,16,12,128]{3,1,2,0:T(8,128)(2,1)} %copy.153), calls=%async_computation.8 | async-start | bytes 1572864 | tf_op jit(solution)/shard_map/all_to_all | solution.py:99
  145.9 5.0 %fusion.40 = (f32[6,512]{1,0:T(8,128)S(1)}, f32[6,512,512]{1,2,0:T(8,128)}) fusion(pred[512,512]{0,1:T(8,128)(4,1)S(1)} %iota_compare_fusion, bf16[6,512,128]{2,1,0:T(8,128)(2,1)S(1)} %bitcast.230, bf16[6,512,128]{2,1,0:T(8,128)(2,1)S(1)} %bitcast.192), kind=kOutput, calls=%fused_computation.65 | convolution fusion | flops 408945152 | bytes 8138752 | tf_op jit(solution)/shard_map/sub | solution.py:22
  150.9 5.4 %fusion.6 = bf16[6,512,512]{1,2,0:T(8,128)(2,1)} fusion(f32[6,512,512]{1,2,0:T(8,128)} %get-tuple-element.14, f32[6,512]{1,0:T(8,128)S(1)} %get-tuple-element.13), kind=kLoop, calls=%fused_computation.13 | loop fusion | flops 3145728 | bytes 9449472 | tf_op jit(solution)/shard_map/convert_element_type | solution.py:24
  156.3 7.8 %all-to-all-done.8 = bf16[16,16,12,128]{3,1,2,0:T(8,128)(2,1)} async-done(((bf16[16,16,12,128]{3,1,2,0:T(8,128)(2,1)}), bf16[16,16,12,128]{3,1,2,0:T(8,128)(2,1)}, u32[]{:S(2)}, u32[]{:S(2)}) %all-to-all-start.8) | async-done | bytes 786464 | tf_op jit(solution)/shard_map/all_to_all | solution.py:99
  164.1 4.7 %all-to-all-start.7 = ((bf16[16,16,12,128]{3,1,2,0:T(8,128)(2,1)}), bf16[16,16,12,128]{3,1,2,0:T(8,128)(2,1)S(1)}, u32[]{:S(2)}, u32[]{:S(2)}) async-start(bf16[16,16,12,128]{3,1,2,0:T(8,128)(2,1)} %copy.152), calls=%async_computation.7 | async-start | bytes 1572864 | tf_op jit(solution)/shard_map/all_to_all | solution.py:100
  172.6 3.8 %multiply_convert_fusion = bf16[6,512,512]{1,2,0:T(8,128)(2,1)S(1)} fusion(f32[6,512]{1,0:T(8,128)S(1)} %multiply_reduce_fusion.1, bf16[6,512,128]{2,1,0:T(8,128)(2,1)S(1)} %bitcast.232, bf16[6,512,128]{2,1,0:T(8,128)(2,1)S(1)} %bitcast.235, f32[6,512,512]{1,2,0:T(8,128)} %get-tuple-element.14, f32[6,512]{1,0:T(8,128)S(1)} %get-tuple-element.13), kind=kOutput, calls=%fused_computation.2 | convolution fusion | flops 408944640 | bytes 11034624 | tf_op jit(solution)/shard_map/gqe,gke->gqk/dot_general | solution.py:29
  179.6 10.5 %all-to-all-done.7 = bf16[16,16,12,128]{3,1,2,0:T(8,128)(2,1)S(1)} async-done(((bf16[16,16,12,128]{3,1,2,0:T(8,128)(2,1)}), bf16[16,16,12,128]{3,1,2,0:T(8,128)(2,1)S(1)}, u32[]{:S(2)}, u32[]{:S(2)}) %all-to-all-start.7) | async-done | bytes 786464 | tf_op jit(solution)/shard_map/all_to_all | solution.py:100
  190.0 5.7 %all-to-all-start.4 = ((bf16[1,6,512,128]{3,1,0,2:T(8,128)(2,1)}), bf16[1,6,512,128]{3,1,0,2:T(8,128)(2,1)S(1)}, u32[]{:S(2)}, u32[]{:S(2)}) async-start(bf16[1,6,512,128]{3,1,0,2:T(8,128)(2,1)} %copy.144), calls=%async_computation.4 | async-start | bytes 2097152 | tf_op jit(solution)/shard_map/all_to_all | solution.py:104
  205.3 5.7 %all-to-all-done.4 = bf16[1,6,512,128]{3,1,0,2:T(8,128)(2,1)S(1)} async-done(((bf16[1,6,512,128]{3,1,0,2:T(8,128)(2,1)}), bf16[1,6,512,128]{3,1,0,2:T(8,128)(2,1)S(1)}, u32[]{:S(2)}, u32[]{:S(2)}) %all-to-all-start.4) | async-done | bytes 786464 | tf_op jit(solution)/shard_map/all_to_all | solution.py:104
  211.0 6.4 %all-to-all-start.10 = ((bf16[1,6,512,128]{3,1,0,2:T(8,128)(2,1)}), bf16[1,6,512,128]{3,1,0,2:T(8,128)(2,1)S(1)}, u32[]{:S(2)}, u32[]{:S(2)}) async-start(bf16[1,6,512,128]{3,1,0,2:T(8,128)(2,1)} %copy.164), calls=%async_computation.10 | async-start | bytes 2097152 | tf_op jit(solution)/shard_map/all_to_all | solution.py:105
  217.4 4.1 %fusion.39 = (f32[16,192]{1,0:T(8,128)S(1)}, f32[16,192,192]{1,2,0:T(8,128)S(1)}) fusion(f32[16,192,192]{1,2,0:T(8,128)} %fusion.21, pred[192,192]{0,1:T(8,128)(4,1)S(1)} %iota_compare_fusion.1), kind=kOutput, calls=%fused_computation.64 | output fusion | flops 3539135 | bytes 4767744 | tf_op jit(solution)/shard_map/sub | solution.py:22
  225.5 7.1 %all-to-all-done.10 = bf16[1,6,512,128]{3,1,0,2:T(8,128)(2,1)S(1)} async-done(((bf16[1,6,512,128]{3,1,0,2:T(8,128)(2,1)}), bf16[1,6,512,128]{3,1,0,2:T(8,128)(2,1)S(1)}, u32[]{:S(2)}, u32[]{:S(2)}) %all-to-all-start.10) | async-done | bytes 786464 | tf_op jit(solution)/shard_map/all_to_all | solution.py:105
  232.6 7.0 %all-to-all-start.12 = ((bf16[1,6,512,128]{3,1,0,2:T(8,128)(2,1)}), bf16[1,6,512,128]{3,1,0,2:T(8,128)(2,1)}, u32[]{:S(2)}, u32[]{:S(2)}) async-start(bf16[1,6,512,128]{3,1,0,2:T(8,128)(2,1)} %copy.171), calls=%async_computation.12 | async-start | bytes 2097152 | tf_op jit(solution)/shard_map/all_to_all | solution.py:106
  245.3 9.6 %all-to-all-done.12 = bf16[1,6,512,128]{3,1,0,2:T(8,128)(2,1)} async-done(((bf16[1,6,512,128]{3,1,0,2:T(8,128)(2,1)}), bf16[1,6,512,128]{3,1,0,2:T(8,128)(2,1)}, u32[]{:S(2)}, u32[]{:S(2)}) %all-to-all-start.12) | async-done | bytes 786464 | tf_op jit(solution)/shard_map/all_to_all | solution.py:106
  255.0 5.1 %all-to-all-start.11 = ((bf16[1,16,192,128]{3,1,0,2:T(8,128)(2,1)}), bf16[1,16,192,128]{3,1,0,2:T(8,128)(2,1)}, u32[]{:S(2)}, u32[]{:S(2)}) async-start(bf16[1,16,192,128]{3,1,0,2:T(8,128)(2,1)} %copy.169), calls=%async_computation.11 | async-start | bytes 1572864 | tf_op jit(solution)/shard_map/all_to_all | solution.py:110
  263.6 18.0 %all-to-all-done.11 = bf16[1,16,192,128]{3,1,0,2:T(8,128)(2,1)} async-done(((bf16[1,16,192,128]{3,1,0,2:T(8,128)(2,1)}), bf16[1,16,192,128]{3,1,0,2:T(8,128)(2,1)}, u32[]{:S(2)}, u32[]{:S(2)}) %all-to-all-start.11) | async-done | bytes 786464 | tf_op jit(solution)/shard_map/all_to_all | solution.py:110
  281.7 4.5 %all-to-all-start.9 = ((bf16[1,16,192,128]{3,1,0,2:T(8,128)(2,1)}), bf16[1,16,192,128]{3,1,0,2:T(8,128)(2,1)S(1)}, u32[]{:S(2)}, u32[]{:S(2)}) async-start(bf16[1,16,192,128]{3,1,0,2:T(8,128)(2,1)} %copy.162), calls=%async_computation.9 | async-start | bytes 1572864 | tf_op jit(solution)/shard_map/all_to_all | solution.py:109
  290.3 17.3 %all-to-all-done.9 = bf16[1,16,192,128]{3,1,0,2:T(8,128)(2,1)S(1)} async-done(((bf16[1,16,192,128]{3,1,0,2:T(8,128)(2,1)}), bf16[1,16,192,128]{3,1,0,2:T(8,128)(2,1)S(1)}, u32[]{:S(2)}, u32[]{:S(2)}) %all-to-all-start.9) | async-done | bytes 786464 | tf_op jit(solution)/shard_map/all_to_all | solution.py:109
  308.5 4.7 %all-to-all-start.13 = ((bf16[1,16,192,128]{3,1,0,2:T(8,128)(2,1)}), bf16[1,16,192,128]{3,1,0,2:T(8,128)(2,1)}, u32[]{:S(2)}, u32[]{:S(2)}) async-start(bf16[1,16,192,128]{3,1,0,2:T(8,128)(2,1)} %copy.176), calls=%async_computation.13 | async-start | bytes 1572864 | tf_op jit(solution)/shard_map/all_to_all | solution.py:111
  322.6 11.9 %all-to-all-done.13 = bf16[1,16,192,128]{3,1,0,2:T(8,128)(2,1)} async-done(((bf16[1,16,192,128]{3,1,0,2:T(8,128)(2,1)}), bf16[1,16,192,128]{3,1,0,2:T(8,128)(2,1)}, u32[]{:S(2)}, u32[]{:S(2)}) %all-to-all-start.13) | async-done | bytes 786464 | tf_op jit(solution)/shard_map/all_to_all | solution.py:111
  (103 shorter events, 78.8 us)
Async XLA Ops:
  3.1 8.7 %copy-start.11 = (bf16[12,32,2048]{2,1,0:T(8,128)(2,1)S(1)}, bf16[12,32,2048]{2,1,0:T(8,128)(2,1)}, u32[]{:S(2)}) copy-start(bf16[12,32,2048]{2,1,0:T(8,128)(2,1)} %param.5) | copy-start | bytes 4718596
  4.4 19.8 %all-to-all-start = ((bf16[16,6,32,128]{3,2,1,0:T(8,128)(2,1)}), bf16[16,6,32,128]{3,2,1,0:T(8,128)(2,1)S(1)}, u32[]{:S(2)}, u32[]{:S(2)}) async-start(bf16[16,6,32,128]{3,2,1,0:T(8,128)(2,1)} %bitcast.1), calls=%async_computation | async-start | bytes 1572864 | tf_op jit(solution)/shard_map/all_to_all | solution.py:90
  24.2 18.7 %all-to-all-start.1 = ((bf16[16,6,32,128]{3,2,1,0:T(8,128)(2,1)}), bf16[16,6,32,128]{3,2,1,0:T(8,128)(2,1)S(1)}, u32[]{:S(2)}, u32[]{:S(2)}) async-start(bf16[16,6,32,128]{3,2,1,0:T(8,128)(2,1)} %bitcast.6), calls=%async_computation.1 | async-start | bytes 1572864 | tf_op jit(solution)/shard_map/all_to_all | solution.py:91
  42.9 18.8 %all-to-all-start.3 = ((bf16[16,6,32,128]{3,2,1,0:T(8,128)(2,1)}), bf16[16,6,32,128]{3,2,1,0:T(8,128)(2,1)S(1)}, u32[]{:S(2)}, u32[]{:S(2)}) async-start(bf16[16,6,32,128]{3,2,1,0:T(8,128)(2,1)} %bitcast.16), calls=%async_computation.3 | async-start | bytes 1572864 | tf_op jit(solution)/shard_map/all_to_all | solution.py:92
  61.6 19.7 %copy-start.3 = (bf16[16,6,32,128]{3,2,1,0:T(8,128)(2,1)}, bf16[16,6,32,128]{3,2,1,0:T(8,128)(2,1)S(1)}, u32[]{:S(2)}) copy-start(bf16[16,6,32,128]{3,2,1,0:T(8,128)(2,1)S(1)} %all-to-all-done.3) | copy-start | bytes 2359300
  61.6 18.8 %all-to-all-start.2 = ((bf16[16,6,32,128]{3,2,1,0:T(8,128)(2,1)}), bf16[16,6,32,128]{3,2,1,0:T(8,128)(2,1)S(1)}, u32[]{:S(2)}, u32[]{:S(2)}) async-start(bf16[16,6,32,128]{3,2,1,0:T(8,128)(2,1)} %bitcast.202), calls=%async_computation.2 | async-start | bytes 1572864 | tf_op jit(solution)/shard_map/all_to_all | solution.py:93
  81.3 30.9 %all-to-all-start.5 = ((bf16[16,16,12,128]{3,1,2,0:T(8,128)(2,1)}), bf16[16,16,12,128]{3,1,2,0:T(8,128)(2,1)S(1)}, u32[]{:S(2)}, u32[]{:S(2)}) async-start(bf16[16,16,12,128]{3,1,2,0:T(8,128)(2,1)} %copy.148), calls=%async_computation.5 | async-start | bytes 1572864 | tf_op jit(solution)/shard_map/all_to_all | solution.py:97
  112.2 90.8 %copy-start = (bf16[16,16,12,128]{3,1,2,0:T(8,128)(2,1)}, bf16[16,16,12,128]{3,1,2,0:T(8,128)(2,1)S(1)}, u32[]{:S(2)}) copy-start(bf16[16,16,12,128]{3,1,2,0:T(8,128)(2,1)S(1)} %all-to-all-done.5) | copy-start | bytes 2359300
  112.2 25.9 %all-to-all-start.6 = ((bf16[16,16,12,128]{3,1,2,0:T(8,128)(2,1)}), bf16[16,16,12,128]{3,1,2,0:T(8,128)(2,1)S(1)}, u32[]{:S(2)}, u32[]{:S(2)}) async-start(bf16[16,16,12,128]{3,1,2,0:T(8,128)(2,1)} %copy.149), calls=%async_computation.6 | async-start | bytes 1572864 | tf_op jit(solution)/shard_map/all_to_all | solution.py:98
  116.7 2.5 copy-start.9
  138.1 26.0 %all-to-all-start.8 = ((bf16[16,16,12,128]{3,1,2,0:T(8,128)(2,1)}), bf16[16,16,12,128]{3,1,2,0:T(8,128)(2,1)}, u32[]{:S(2)}, u32[]{:S(2)}) async-start(bf16[16,16,12,128]{3,1,2,0:T(8,128)(2,1)} %copy.153), calls=%async_computation.8 | async-start | bytes 1572864 | tf_op jit(solution)/shard_map/all_to_all | solution.py:99
  142.8 1.2 copy-start.4
  142.8 2.2 copy-start.6
  144.0 2.0 copy-start.15
  164.1 25.9 %all-to-all-start.7 = ((bf16[16,16,12,128]{3,1,2,0:T(8,128)(2,1)}), bf16[16,16,12,128]{3,1,2,0:T(8,128)(2,1)S(1)}, u32[]{:S(2)}, u32[]{:S(2)}) async-start(bf16[16,16,12,128]{3,1,2,0:T(8,128)(2,1)} %copy.152), calls=%async_computation.7 | async-start | bytes 1572864 | tf_op jit(solution)/shard_map/all_to_all | solution.py:100
  168.8 3.8 %copy-start.16 = (bf16[1,6,16,32,128]{4,3,2,1,0:T(8,128)(2,1)S(1)}, bf16[1,6,16,32,128]{4,3,2,1,0:T(8,128)(2,1)}, u32[]{:S(2)}) copy-start(bf16[1,6,16,32,128]{4,3,2,1,0:T(8,128)(2,1)} %copy.136) | copy-start | bytes 2359300
  168.8 3.8 %copy-start.18 = (bf16[1,6,16,32,128]{4,3,2,1,0:T(8,128)(2,1)S(1)}, bf16[1,6,16,32,128]{4,3,2,1,0:T(8,128)(2,1)}, u32[]{:S(2)}) copy-start(bf16[1,6,16,32,128]{4,3,2,1,0:T(8,128)(2,1)} %copy.138) | copy-start | bytes 2359300
  176.4 1.6 copy-start.2
  190.0 8.9 %copy-start.13 = (bf16[16,16,12,128]{3,1,2,0:T(8,128)(2,1)}, bf16[16,16,12,128]{3,1,2,0:T(8,128)(2,1)S(1)}, u32[]{:S(2)}) copy-start(bf16[16,16,12,128]{3,1,2,0:T(8,128)(2,1)S(1)} %all-to-all-done.7) | copy-start | bytes 2359300
  190.0 20.9 %all-to-all-start.4 = ((bf16[1,6,512,128]{3,1,0,2:T(8,128)(2,1)}), bf16[1,6,512,128]{3,1,0,2:T(8,128)(2,1)S(1)}, u32[]{:S(2)}, u32[]{:S(2)}) async-start(bf16[1,6,512,128]{3,1,0,2:T(8,128)(2,1)} %copy.144), calls=%async_computation.4 | async-start | bytes 2097152 | tf_op jit(solution)/shard_map/all_to_all | solution.py:104
  195.7 4.8 %copy-start.10 = (bf16[6,512,512]{1,2,0:T(8,128)(2,1)S(1)}, bf16[6,512,512]{1,2,0:T(8,128)(2,1)}, u32[]{:S(2)}) copy-start(bf16[6,512,512]{1,2,0:T(8,128)(2,1)} %fusion.6) | copy-start | bytes 9437188
  195.7 4.8 %copy-start.17 = (bf16[1,6,16,32,128]{4,3,2,1,0:T(8,128)(2,1)S(1)}, bf16[1,6,16,32,128]{4,3,2,1,0:T(8,128)(2,1)}, u32[]{:S(2)}) copy-start(bf16[1,6,16,32,128]{4,3,2,1,0:T(8,128)(2,1)} %copy.136) | copy-start | bytes 2359300
  211.0 21.6 %all-to-all-start.10 = ((bf16[1,6,512,128]{3,1,0,2:T(8,128)(2,1)}), bf16[1,6,512,128]{3,1,0,2:T(8,128)(2,1)S(1)}, u32[]{:S(2)}, u32[]{:S(2)}) async-start(bf16[1,6,512,128]{3,1,0,2:T(8,128)(2,1)} %copy.164), calls=%async_computation.10 | async-start | bytes 2097152 | tf_op jit(solution)/shard_map/all_to_all | solution.py:105
  217.3 5.7 %copy-start.14 = (bf16[16,16,12,128]{3,1,2,0:T(8,128)(2,1)S(1)}, bf16[16,16,12,128]{3,1,2,0:T(8,128)(2,1)}, u32[]{:S(2)}) copy-start(bf16[16,16,12,128]{3,1,2,0:T(8,128)(2,1)} %copy-done.13) | copy-start | bytes 2359300
  221.5 1.6 copy-start.19
  232.6 22.4 %all-to-all-start.12 = ((bf16[1,6,512,128]{3,1,0,2:T(8,128)(2,1)}), bf16[1,6,512,128]{3,1,0,2:T(8,128)(2,1)}, u32[]{:S(2)}, u32[]{:S(2)}) async-start(bf16[1,6,512,128]{3,1,0,2:T(8,128)(2,1)} %copy.171), calls=%async_computation.12 | async-start | bytes 2097152 | tf_op jit(solution)/shard_map/all_to_all | solution.py:106
  239.6 3.2 copy-start.1
  242.8 1.1 copy-start.12
  255.0 26.7 %all-to-all-start.11 = ((bf16[1,16,192,128]{3,1,0,2:T(8,128)(2,1)}), bf16[1,16,192,128]{3,1,0,2:T(8,128)(2,1)}, u32[]{:S(2)}, u32[]{:S(2)}) async-start(bf16[1,16,192,128]{3,1,0,2:T(8,128)(2,1)} %copy.169), calls=%async_computation.11 | async-start | bytes 1572864 | tf_op jit(solution)/shard_map/all_to_all | solution.py:110
  281.7 25.9 %all-to-all-start.9 = ((bf16[1,16,192,128]{3,1,0,2:T(8,128)(2,1)}), bf16[1,16,192,128]{3,1,0,2:T(8,128)(2,1)S(1)}, u32[]{:S(2)}, u32[]{:S(2)}) async-start(bf16[1,16,192,128]{3,1,0,2:T(8,128)(2,1)} %copy.162), calls=%async_computation.9 | async-start | bytes 1572864 | tf_op jit(solution)/shard_map/all_to_all | solution.py:109
  308.5 26.0 %all-to-all-start.13 = ((bf16[1,16,192,128]{3,1,0,2:T(8,128)(2,1)}), bf16[1,16,192,128]{3,1,0,2:T(8,128)(2,1)}, u32[]{:S(2)}, u32[]{:S(2)}) async-start(bf16[1,16,192,128]{3,1,0,2:T(8,128)(2,1)} %copy.176), calls=%async_computation.13 | async-start | bytes 1572864 | tf_op jit(solution)/shard_map/all_to_all | solution.py:111
  315.3 4.8 %copy-start.8 = (bf16[1,16,192,128]{3,1,0,2:T(8,128)(2,1)S(1)}, bf16[1,16,192,128]{3,1,0,2:T(8,128)(2,1)}, u32[]{:S(2)}) copy-start(bf16[1,16,192,128]{3,1,0,2:T(8,128)(2,1)} %copy-done.7) | copy-start | bytes 2359300
  (2 other events, 1.8 us)
where the time goes:
time: 346 us; the launch traced here: 343 us
  waiting for transfers between devices  162 us (47%)
  starting transfers between devices  83.2 us (24%)
  local copies, waits for them, and re-layouts  51.7 us (15%)
  matrix products  31.1 us (9%)
  other arithmetic  14.2 us (4%)
    all_to_all x1, waiting for transfers between devices, body(): lax.all_to_all(col_query, 'row', split_axis=0, concat_axis=2, tiled=True)  19.2 us
    all_to_all x1, waiting for transfers between devices, body(): lax.all_to_all(col_results[1], 'row', split_axis=2, concat_axis=0, tiled=...  18 us
    all_to_all x1, waiting for transfers between devices, body(): lax.all_to_all(col_key, 'row', split_axis=0, concat_axis=2, tiled=True)  17.6 us
    all_to_all x1, waiting for transfers between devices, body(): lax.all_to_all(col_results[0], 'row', split_axis=2, concat_axis=0, tiled=...  17.3 us
    all_to_all x1, waiting for transfers between devices, body(): lax.all_to_all(col_results[2], 'row', split_axis=2, concat_axis=0, tiled=...  11.9 us
    all_to_all x1, waiting for transfers between devices, body(): lax.all_to_all(col_grad, 'row', split_axis=0, concat_axis=2, tiled=True)  10.5 us
    all_to_all x1, waiting for transfers between devices, body(): lax.all_to_all(row_query, 'col', split_axis=0, concat_axis=2, tiled=True)  10.1 us
    all_to_all x1, waiting for transfers between devices, body(): lax.all_to_all(row_grad, 'col', split_axis=0, concat_axis=2, tiled=True)  9.93 us
  transfers between devices with their start and end apart: 14, of which 14 were waited for; matrix products, arithmetic and copies ran while one was open for 23% of the time, Pallas kernels for 0%

commit v1 on v0

v1 whole, which is shorter than its diff:
```python
import functools
import math

import jax
import jax.numpy as jnp
from jax import lax
from jax.experimental import pallas as pl
from jax.experimental.pallas import tpu as pltpu
from jax.sharding import PartitionSpec as P

MESH = pl.DeviceIdType.MESH
HEAD_DIM = 128
RING = 8
FACTOR = 1.0 / math.sqrt(HEAD_DIM)
LOG2E = math.log2(math.e)
BF16, F32 = jnp.bfloat16, jnp.float32

KEY, VALUE, QUERY, GRAD = range(4)
DKEY, DVALUE, DQUERY = range(3)
COL_CHUNKS = 2
ROW_CHUNKS = 2


def attend_back(keys, values, queries, grads, causal_from):
    key_count, query_count = keys.shape[0], queries.shape[0]
    contract_last = (((1,), (1,)), ((), ()))
    raw = lax.dot_general(keys, queries, contract_last, preferred_element_type=F32)
    key_at = lax.broadcasted_iota(jnp.int32, (key_count, query_count), 0)
    query_at = lax.broadcasted_iota(jnp.int32, (key_count, query_count), 1)
    raw = jnp.where(key_at <= query_at + causal_from, raw, -jnp.inf)
    highest = jnp.max(raw, axis=0, keepdims=True)
    weights = jnp.exp2((raw - highest) * (FACTOR * LOG2E))
    probs = weights * (1.0 / jnp.sum(weights, axis=0, keepdims=True))
    probs_low = probs.astype(BF16)
    grad_weights = lax.dot_general(values, grads, contract_last, preferred_element_type=F32)
    correction = jnp.sum(probs_low.astype(F32) * grad_weights, axis=0, keepdims=True)
    grad_scores = (probs * (grad_weights - correction)).astype(BF16)
    grad_values = jnp.dot(probs_low, grads, preferred_element_type=F32)
    grad_keys = jnp.dot(grad_scores, queries, preferred_element_type=F32) * FACTOR
    grad_queries = (
        lax.dot_general(grad_scores, keys, (((0,), (0,)), ((), ())), preferred_element_type=F32)
        * FACTOR
    )
    return grad_keys, grad_values, grad_queries


def kernel(
    q_ref, k_ref, v_ref, g_ref, dq_ref, dk_ref, dv_ref,
    c_in, c_low, c_out, c_part, c_back, f_in, f_out,
    r_in, r_low, r_out, r_part, r_back, r_sum,
    ci_send, ci_recv, cl_send, cl_recv, cb_send, cb_recv, co_send, co_recv,
    ri_send, ri_recv, rl_send, rl_recv, rb_send, rb_recv, ro_send, ro_recv,
):
    inputs = (k_ref, v_ref, q_ref, g_ref)
    outputs = (dk_ref, dv_ref, dq_ref)
    row_count, col_count, width = q_ref.shape
    half = width // 2
    col_step = col_count // COL_CHUNKS
    row_step = row_count // ROW_CHUNKS
    col_len = row_count * RING
    row_len = col_count * RING

    row = lax.axis_index("row")
    col = lax.axis_index("col")
    x_lo, z = row // RING, lax.rem(row, RING)
    x_hi, j = col // RING, lax.rem(col, RING)

    def z_peer(at):
        return (x_lo * RING + at, col)

    def j_peer(at):
        return (row, x_hi * RING + at)

    lo_peer = ((1 - x_lo) * RING + z, col)
    hi_peer = (row, (1 - x_hi) * RING + j)

    def others(start, step):
        def at(d, carry):
            step(lax.rem(start + d, RING))
            return carry

        lax.fori_loop(1, RING, at, 0)

    barrier = pltpu.get_barrier_semaphore()

    def greet(target):
        pl.semaphore_signal(barrier, inc=1, device_id=target, device_id_type=MESH)

    others(z, lambda at: greet(z_peer(at)))
    others(j, lambda at: greet(j_peer(at)))
    greet(lo_peer)
    greet(hi_peer)
    pl.semaphore_wait(barrier, 2 * RING)

    def lanes(first):
        return pl.ds(pl.multiple_of(first, HEAD_DIM), HEAD_DIM)

    def send(src, dst, send_sem, recv_sem, target):
        pltpu.make_async_remote_copy(
            src_ref=src, dst_ref=dst, send_sem=send_sem, recv_sem=recv_sem,
            device_id=target, device_id_type=MESH,
        ).start()

    def take(ref, sem):
        pltpu.make_async_copy(ref, ref, sem).wait()

    def c_rows(at):
        return pl.ds(at * row_count, row_count)

    def r_cols(at):
        return pl.ds(pl.multiple_of(at * col_count, col_count), col_count)

    def c_send_in(t, n):
        def src(at):
            return inputs[t].at[:, pl.ds(n * col_step, col_step), lanes(half + at * HEAD_DIM)]

        dst = c_in.at[t, n, c_rows(z)]
        others(z, lambda at: send(src(at), dst, ci_send.at[t, n], ci_recv.at[t, n], z_peer(at)))
        pltpu.make_async_copy(src(z), dst, ci_recv.at[t, n]).start()

    def c_send_out(o, n):
        dst = outputs[o].at[:, pl.ds(n * col_step, col_step), lanes(half + z * HEAD_DIM)]

        def src(at):
            return c_out.at[o, n, c_rows(at)]

        others(z, lambda at: send(src(at), dst, co_send.at[o, n], co_recv.at[o, n], z_peer(at)))
        pltpu.make_async_copy(src(z), dst, co_recv.at[o, n]).start()

    def r_span(n):
        return pl.ds(n * row_step, row_step)

    def r_send_in(t, n):
        def src(at):
            return inputs[t].at[r_span(n), :, lanes(at * HEAD_DIM)]

        dst = r_in.at[t, r_span(n), r_cols(j)]
        others(j, lambda at: send(src(at), dst, ri_send.at[t, n], ri_recv.at[t, n], j_peer(at)))
        pltpu.make_async_copy(src(j), dst, ri_recv.at[t, n]).start()

    def r_send_out(o, n):
        dst = outputs[o].at[r_span(n), :, lanes(j * HEAD_DIM)]

        def src(at):
            return r_out.at[o, r_span(n), r_cols(at)]

        others(j, lambda at: send(src(at), dst, ro_send.at[o, n], ro_recv.at[o, n], j_peer(at)))
        pltpu.make_async_copy(src(j), dst, ro_recv.at[o, n]).start()

    def c_relay(n):
        @pl.when(x_lo == 0)
        def _():
            for t in (KEY, VALUE):
                take(c_in.at[t, n], ci_recv.at[t, n])
                send(c_in.at[t, n], c_low.at[t, n], cl_send.at[t, n], cl_recv.at[t, n], lo_peer)

    def r_relay(n):
        @pl.when(x_hi == 0)
        def _():
            for t in (KEY, VALUE):
                take(r_in.at[t, r_span(n)], ri_recv.at[t, n])
                send(
                    r_in.at[t, r_span(n)], r_low.at[t, r_span(n)],
                    rl_send.at[t, n], rl_recv.at[t, n], hi_peer,
                )

    def spread(slot, ref):
        f_in[slot] = ref[...].astype(F32).reshape(col_len * col_step, HEAD_DIM)

    def packed(n, slot):
        return f_out[n, slot].reshape(col_len, col_step, HEAD_DIM)

    def c_work(n):
        def column(slot, c):
            return f_in[slot, pl.ds(c, col_len, stride=col_step), :].astype(BF16)

        def put(slot, c, value):
            f_out[n, slot, pl.ds(c, col_len, stride=col_step), :] = value

        @pl.when(x_lo == 0)
        def _():
            for t in (QUERY, GRAD):
                take(c_in.at[t, n], ci_recv.at[t, n])
            for t in range(4):
                spread(t, c_in.at[t, n])

            def item(c, carry):
                parts = attend_back(
                    column(KEY, c), column(VALUE, c), column(QUERY, c), column(GRAD, c), 0
                )
                for o in range(3):
                    put(o, c, parts[o])
                return carry

            lax.fori_loop(0, col_step, item, 0, unroll=2)
            c_out[DQUERY, n] = packed(n, DQUERY).astype(BF16)
            c_send_out(DQUERY, n)

        @pl.when(x_lo == 1)
        def _():
            for t in range(4):
                take(c_in.at[t, n], ci_recv.at[t, n])
                spread(t, c_in.at[t, n])
            for t in (KEY, VALUE):
                take(c_low.at[t, n], cl_recv.at[t, n])
                spread(4 + t, c_low.at[t, n])

            def item(c, carry):
                keys = jnp.concatenate([column(4 + KEY, c), column(KEY, c)], axis=0)
                values = jnp.concatenate([column(4 + VALUE, c), column(VALUE, c)], axis=0)
                parts = attend_back(keys, values, column(QUERY, c), column(GRAD, c), col_len)
                put(DQUERY, c, parts[DQUERY])
                for o in (DKEY, DVALUE):
                    put(o, c, parts[o][col_len:])
                    put(3 + o, c, parts[o][:col_len])
                return carry

            lax.fori_loop(0, col_step, item, 0, unroll=2)
            for o in (DKEY, DVALUE):
                c_part[o, n] = packed(n, 3 + o).astype(BF16)
                send(c_part.at[o, n], c_back.at[o, n], cb_send.at[o, n], cb_recv.at[o, n], lo_peer)
            for o in (DQUERY, DKEY, DVALUE):
                c_out[o, n] = packed(n, o).astype(BF16)
                c_send_out(o, n)

    def c_finish(n):
        @pl.when(x_lo == 0)
        def _():
            for o in (DKEY, DVALUE):
                take(c_back.at[o, n], cb_recv.at[o, n])
                c_out[o, n] = (packed(n, o) + c_back[o, n].astype(F32)).astype(BF16)
                c_send_out(o, n)

    tile = row_len // 2

    def r_work(n):
        first = n * row_step

        @pl.when(x_hi == 0)
        def _():
            for t in (QUERY, GRAD):
                take(r_in.at[t, r_span(n)], ri_recv.at[t, n])

            def item(i, carry):
                at = first + i
                for o in (DKEY, DVALUE):
                    r_sum[o, at, tile:] = jnp.zeros((tile, HEAD_DIM), F32)
                for part in range(2):
                    seen = (part + 1) * tile
                    span = slice(part * tile, seen)
                    parts = attend_back(
                        r_in[KEY, at, :seen], r_in[VALUE, at, :seen],
                        r_in[QUERY, at, span], r_in[GRAD, at, span], part * tile,
                    )
                    for o in (DKEY, DVALUE):
                        if part == 0:
                            r_sum[o, at, :seen] = parts[o]
                        else:
                            r_sum[o, at, :seen] += parts[o]
                    r_out[DQUERY, at, span] = parts[DQUERY].astype(BF16)
                return carry

            lax.fori_loop(0, row_step, item, 0)
            r_send_out(DQUERY, n)

        @pl.when(x_hi == 1)
        def _():
            for t in range(4):
                take(r_in.at[t, r_span(n)], ri_recv.at[t, n])
            for t in (KEY, VALUE):
                take(r_low.at[t, r_span(n)], rl_recv.at[t, n])

            def item(i, carry):
                at = first + i
                sums = []
                for part in range(2):
                    seen = (part + 1) * tile
                    span = slice(part * tile, seen)
                    keys = jnp.concatenate([r_low[KEY, at], r_in[KEY, at, :seen]], axis=0)
                    values = jnp.concatenate([r_low[VALUE, at], r_in[VALUE, at, :seen]], axis=0)
                    parts = attend_back(
                        keys, values, r_in[QUERY, at, span], r_in[GRAD, at, span],
                        row_len + part * tile,
                    )
                    r_out[DQUERY, at, span] = parts[DQUERY].astype(BF16)
                    sums.append(parts)
                for o in (DKEY, DVALUE):
                    both = row_len + tile
                    total = sums[0][o] + sums[1][o][:both]
                    r_part[o, at] = total[:row_len].astype(BF16)
                    r_out[o, at, :tile] = total[row_len:].astype(BF16)
                    r_out[o, at, tile:] = sums[1][o][both:].astype(BF16)
                return carry

            lax.fori_loop(0, row_step, item, 0)
            for o in (DKEY, DVALUE):
                send(
                    r_part.at[o, r_span(n)], r_back.at[o, r_span(n)],
                    rb_send.at[o, n], rb_recv.at[o, n], hi_peer,
                )
            for o in (DQUERY, DKEY, DVALUE):
                r_send_out(o, n)

    def r_finish(n):
        @pl.when(x_hi == 0)
        def _():
            span = r_span(n)
            for o in (DKEY, DVALUE):
                take(r_back.at[o, span], rb_recv.at[o, n])
                r_out[o, span] = (r_sum[o, span] + r_back[o, span].astype(F32)).astype(BF16)
                r_send_out(o, n)

    for n in range(2):
        for t in (KEY, VALUE, QUERY, GRAD):
            c_send_in(t, n)
            r_send_in(t, n)

    r_relay(0)
    c_relay(0)
    r_work(0)
    r_relay(1)
    c_work(0)
    c_relay(1)
    r_work(1)
    r_finish(0)
    c_finish(0)
    c_work(1)
    r_finish(1)
    c_finish(1)

    sent = (RING - 1) * row_count
    sent_cols = (RING - 1) * col_count
    for n in range(2):
        for t in range(4):
            take(c_in.at[t, n, :sent], ci_send.at[t, n])
            take(r_in.at[t, r_span(n), :sent_cols], ri_send.at[t, n])
        for o in range(3):
            take(c_out.at[o, n, :sent], co_send.at[o, n])
            take(r_out.at[o, r_span(n), :sent_cols], ro_send.at[o, n])
            take(c_out.at[o, n], co_recv.at[o, n])
            take(r_out.at[o, r_span(n)], ro_recv.at[o, n])
        for t in (KEY, VALUE):
            @pl.when(x_lo == 0)
            def _():
                take(c_in.at[t, n], cl_send.at[t, n])

            @pl.when(x_lo == 1)
            def _():
                take(c_part.at[t, n], cb_send.at[t, n])

            @pl.when(x_hi == 0)
            def _():
                take(r_in.at[t, r_span(n)], rl_send.at[t, n])

            @pl.when(x_hi == 1)
            def _():
                take(r_part.at[t, r_span(n)], rb_send.at[t, n])


def body(queries, key_vectors, value_vectors, grad_output):
    row_count, col_count, width = queries.shape
    col_step = col_count // COL_CHUNKS
    col_len, row_len = row_count * RING, col_count * RING
    c_shape = (COL_CHUNKS, col_len, col_step, HEAD_DIM)
    r_shape = (row_count, row_len, HEAD_DIM)
    flat = (col_len * col_step, HEAD_DIM)
    dma = pltpu.SemaphoreType.DMA
    scratch = [
        pltpu.VMEM((4, *c_shape), BF16),
        pltpu.VMEM((2, *c_shape), BF16),
        pltpu.VMEM((3, *c_shape), BF16),
        pltpu.VMEM((2, *c_shape), BF16),
        pltpu.VMEM((2, *c_shape), BF16),
        pltpu.VMEM((6, *flat), F32),
        pltpu.VMEM((COL_CHUNKS, 5, *flat), F32),
        pltpu.VMEM((4, *r_shape), BF16),
        pltpu.VMEM((2, *r_shape), BF16),
        pltpu.VMEM((3, *r_shape), BF16),
        pltpu.VMEM((2, *r_shape), BF16),
        pltpu.VMEM((2, *r_shape), BF16),
        pltpu.VMEM((2, *r_shape), F32),
    ]
    for chunks in (COL_CHUNKS, ROW_CHUNKS):
        for arrays in (4, 2, 2, 3):
            scratch += [dma((arrays, chunks)), dma((arrays, chunks))]
    shape = jax.ShapeDtypeStruct(queries.shape, BF16)
    return pl.pallas_call(
        kernel,
        out_shape=(shape, shape, shape),
        in_specs=[pl.BlockSpec(memory_space=pl.ANY)] * 4,
        out_specs=[pl.BlockSpec(memory_space=pl.ANY)] * 3,
        scratch_shapes=scratch,
        compiler_params=pltpu.CompilerParams(
            collective_id=0, has_side_effects=True, vmem_limit_bytes=56 * 2**20
        ),
    )(queries, key_vectors, value_vectors, grad_output)


def solution(mesh):
    placed = P("row", "col", None)
    return jax.shard_map(
        body,
        mesh=mesh,
        in_specs=(placed,) * 4,
        out_specs=(placed,) * 3,
        check_vma=False,
    )
```

time: 346 us -> 137 us (0.40)
  waiting for transfers between devices: 162 us -> 0 us
  Pallas kernels: 0 us -> 130 us
  starting transfers between devices: 83.2 us -> 0 us
  local copies, waits for them, and re-layouts: 51.7 us -> 5.97 us
  matrix products: 31.1 us -> 0 us
  other arithmetic: 14.2 us -> 0 us
    all_to_all x14 -> x0, waiting for transfers between devices: 162 us -> none  [the longest x1 19.2 us: body(): lax.all_to_all(col_query, 'row', split_axis=0, concat_axis=2, tiled=True)]
    pallas_call x0 -> x1, Pallas kernels: none -> 130 us  [body(): pl.pallas_call(kernel, out_shape=(shape, shape, shape), in_specs=[pl.Bloc...]
    all_to_all x14 -> x0, starting transfers between devices: 83.2 us -> none  [the longest x1 9.34 us: body(): lax.all_to_all(col_query, 'row', split_axis=0, concat_axis=2, tiled=True)]
    dot_general x11 -> x0, matrix products: 26.1 us -> none  [the longest x2 6.94 us: attend_back(): jnp.einsum('gqe,gke->gqk', grad_block, value_block, preferred_element_typ...]
    reshape x10 -> x0, local copies, waits for them, and re-layouts: 10.8 us -> none  [the longest x3 4.99 us: col_layout(): shaped.transpose(2, 0, 1, 3).reshape(row_count, col_count, half_width)]
    all_to_all x13 -> x0, local copies, waits for them, and re-layouts: 10.2 us -> none  [the longest x1 2.2 us: body(): lax.all_to_all(col_results[2], 'row', split_axis=2, concat_axis=0, tiled=...]
    broadcast_in_dim x6 -> x0, local copies, waits for them, and re-layouts: 8.71 us -> none  [item_block(): return (outcome[0][None], outcome[1][None], outcome[2][None])]
    slice x4 -> x0, local copies, waits for them, and re-layouts: 8.29 us -> none  [row_items(): array[:, :, :half_width].reshape(row_count, col_count, heads_half, HEAD_DIM)]
  transfers between devices with their start and end apart: 14 -> 0, of which waited for: 14 -> 0; matrix products, arithmetic and copies ran while one was open for 23% -> 0% of each run, Pallas kernels for 0% -> 0%
where the time goes in v1:
time: 137 us; the launch traced here: 136 us
  Pallas kernels  130 us (95%)
  local copies, waits for them, and re-layouts  5.97 us (4%)
    pallas_call x1, Pallas kernels, body(): pl.pallas_call(kernel, out_shape=(shape, shape, shape), in_specs=[pl.Bloc...  130 us
    unnamed x7, local copies, waits for them, and re-layouts  5.97 us

profile of v1, /device:TPU:4, one launch (start us, length us, event | category | flops | bytes accessed | tf_op | source)
XLA Modules:
  0.0 136.3 jit_solution(8945694279453685549)
XLA Ops:
  0.6 129.7 %shard_map.67 = (bf16[12,32,2048]{2,1,0:T(8,128)(2,1)}, bf16[12,32,2048]{2,1,0:T(8,128)(2,1)}, bf16[12,32,2048]{2,1,0:T(8,128)(2,1)}) custom-call(bf16[12,32,2048]{2,1,0:T(8,128)(2,1)} %q_ref.1, bf16[12,32,2048]{2,1,0:T(8,128)(2,1)} %k_ref.1, bf16[12,32,2048]{2,1,0:T(8,128)(2,1)} %v_ref.1, bf16[12,32,2048]{2,1,0:T(8,128)(2,1)} %g_ref.1), custom_call_target="tpu_custom_call" | custom-call | tf_op jit(solution)/shard_map/pallas_call | solution.py:387
  130.3 0.0 copy-start.1
  130.4 2.8 %copy.10 = bf16[12,32,2048]{2,1,0:T(8,128)(2,1)} copy(bf16[12,32,2048]{2,1,0:T(8,128)(2,1)} %get-tuple-element.6) | data formatting | bytes 3145728
  133.2 0.0 copy-done.1
  133.2 0.0 copy-start
  133.2 1.1 copy.11
  134.4 0.8 copy-done
  135.2 1.1 copy.12
Async XLA Ops:
  130.3 2.9 %copy-start.1 = (bf16[12,32,2048]{2,1,0:T(8,128)(2,1)S(1)}, bf16[12,32,2048]{2,1,0:T(8,128)(2,1)}, u32[]{:S(2)}) copy-start(bf16[12,32,2048]{2,1,0:T(8,128)(2,1)} %get-tuple-element.7) | copy-start | bytes 4718596
  133.2 2.0 %copy-start = (bf16[12,32,2048]{2,1,0:T(8,128)(2,1)S(1)}, bf16[12,32,2048]{2,1,0:T(8,128)(2,1)}, u32[]{:S(2)}) copy-start(bf16[12,32,2048]{2,1,0:T(8,128)(2,1)} %get-tuple-element.8) | copy-start | bytes 4718596

commit v2 on v1

--- a/solution.py
+++ b/solution.py
@@ -355,6 +355,15 @@
             @pl.when(x_hi == 1)
             def _():
                 take(r_part.at[t, r_span(n)], rb_send.at[t, n])
+
+
+def hand_out(*refs):
+    sems = refs[-1]
+    copies = [pltpu.make_async_copy(refs[o], refs[3 + o], sems.at[o]) for o in range(3)]
+    for copy in copies:
+        copy.start()
+    for copy in copies:
+        copy.wait()
 
 
 def body(queries, key_vectors, value_vectors, grad_output):
@@ -384,16 +393,24 @@
         for arrays in (4, 2, 2, 3):
             scratch += [dma((arrays, chunks)), dma((arrays, chunks))]
     shape = jax.ShapeDtypeStruct(queries.shape, BF16)
-    return pl.pallas_call(
+    grads = pl.pallas_call(
         kernel,
         out_shape=(shape, shape, shape),
-        in_specs=[pl.BlockSpec(memory_space=pl.ANY)] * 4,
+        in_specs=[pl.BlockSpec(memory_space=pltpu.HBM)] * 4,
         out_specs=[pl.BlockSpec(memory_space=pl.ANY)] * 3,
         scratch_shapes=scratch,
         compiler_params=pltpu.CompilerParams(
-            collective_id=0, has_side_effects=True, vmem_limit_bytes=56 * 2**20
+            collective_id=0, has_side_effects=True, vmem_limit_bytes=48 * 2**20
         ),
     )(queries, key_vectors, value_vectors, grad_output)
+    return pl.pallas_call(
+        hand_out,
+        out_shape=(shape, shape, shape),
+        in_specs=[pl.BlockSpec(memory_space=pl.ANY)] * 3,
+        out_specs=[pl.BlockSpec(memory_space=pltpu.HBM)] * 3,
+        scratch_shapes=[dma((3,))],
+        compiler_params=pltpu.CompilerParams(vmem_limit_bytes=8 * 2**20),
+    )(*grads)
 
 
 def solution(mesh):

time: 137 us -> 133 us (0.971)
  local copies, waits for them, and re-layouts: 5.97 us -> 0 us
  Pallas kernels: 130 us -> 132 us
    unnamed x7 -> x0, local copies, waits for them, and re-layouts: 5.97 us -> none
    pallas_call x0 -> x1, Pallas kernels: none -> 2.21 us  [body(): pl.pallas_call(hand_out, out_shape=(shape, shape, shape), in_specs=[pl.Bl...]
where the time goes in v2:
time: 133 us; the launch traced here: 132 us
  Pallas kernels  132 us (99%)
    pallas_call x1, Pallas kernels, body(): pl.pallas_call(kernel, out_shape=(shape, shape, shape), in_specs=[pl.Bloc...  130 us

profile of v2, /device:TPU:4, one launch (start us, length us, event | category | flops | bytes accessed | tf_op | source)
XLA Modules:
  0.0 132.5 jit_solution(63673464462248306)
XLA Ops:
  0.6 129.6 %shard_map.67 = (bf16[12,32,2048]{2,1,0:T(8,128)(2,1)S(1)}, bf16[12,32,2048]{2,1,0:T(8,128)(2,1)S(1)}, bf16[12,32,2048]{2,1,0:T(8,128)(2,1)S(1)}) custom-call(bf16[12,32,2048]{2,1,0:T(8,128)(2,1)} %q_ref.1, bf16[12,32,2048]{2,1,0:T(8,128)(2,1)} %k_ref.1, bf16[12,32,2048]{2,1,0:T(8,128)(2,1)} %v_ref.1, bf16[12,32,2048]{2,1,0:T(8,128)(2,1)} %g_ref.1), custom_call_target="tpu_custom_call" | custom-call | tf_op jit(solution)/shard_map/pallas_call | solution.py:396
  130.2 2.2 %shard_map.68 = (bf16[12,32,2048]{2,1,0:T(8,128)(2,1)}, bf16[12,32,2048]{2,1,0:T(8,128)(2,1)}, bf16[12,32,2048]{2,1,0:T(8,128)(2,1)}) custom-call(bf16[12,32,2048]{2,1,0:T(8,128)(2,1)S(1)} %get-tuple-element.6.refs_0_, bf16[12,32,2048]{2,1,0:T(8,128)(2,1)S(1)} %get-tuple-element.7.refs_1_, bf16[12,32,2048]{2,1,0:T(8,128)(2,1)S(1)} %get-tuple-element.8.refs_2_), custom_call_target="tpu_custom_call" | custom-call | tf_op jit(solution)/shard_map/pallas_call | solution.py:406

commit v3 on v2

--- a/solution.py
+++ b/solution.py
@@ -49,7 +49,7 @@
     c_in, c_low, c_out, c_part, c_back, f_in, f_out,
     r_in, r_low, r_out, r_part, r_back, r_sum,
     ci_send, ci_recv, cl_send, cl_recv, cb_send, cb_recv, co_send, co_recv,
-    ri_send, ri_recv, rl_send, rl_recv, rb_send, rb_recv, ro_send, ro_recv,
+    ri_send, ri_recv, rl_send, rl_recv, rb_send, rb_recv, ro_send, ro_recv, ring_sem, go_sem,
 ):
     inputs = (k_ref, v_ref, q_ref, g_ref)
     outputs = (dk_ref, dv_ref, dq_ref)
@@ -83,14 +83,24 @@
 
     barrier = pltpu.get_barrier_semaphore()
 
-    def greet(target):
-        pl.semaphore_signal(barrier, inc=1, device_id=target, device_id_type=MESH)
-
-    others(z, lambda at: greet(z_peer(at)))
-    others(j, lambda at: greet(j_peer(at)))
-    greet(lo_peer)
-    greet(hi_peer)
-    pl.semaphore_wait(barrier, 2 * RING)
+    def signal(sem, target):
+        pl.semaphore_signal(sem, inc=1, device_id=target, device_id_type=MESH)
+
+    def signal_rings(sem):
+        others(j, lambda at: signal(sem, j_peer(at)))
+        signal(sem, lo_peer)
+        signal(sem, hi_peer)
+
+    others(z, lambda at: signal(barrier, z_peer(at)))
+
+    @pl.when(z == 0)
+    def _():
+        signal_rings(barrier)
+        pl.semaphore_wait(barrier, RING - 1 + RING + 1)
+
+    @pl.when(z != 0)
+    def _():
+        pl.semaphore_wait(barrier, RING - 1)
 
     def lanes(first):
         return pl.ds(pl.multiple_of(first, HEAD_DIM), HEAD_DIM)
@@ -118,14 +128,32 @@
         others(z, lambda at: send(src(at), dst, ci_send.at[t, n], ci_recv.at[t, n], z_peer(at)))
         pltpu.make_async_copy(src(z), dst, ci_recv.at[t, n]).start()
 
-    def c_send_out(o, n):
-        dst = outputs[o].at[:, pl.ds(n * col_step, col_step), lanes(half + z * HEAD_DIM)]
-
-        def src(at):
-            return c_out.at[o, n, c_rows(at)]
-
-        others(z, lambda at: send(src(at), dst, co_send.at[o, n], co_recv.at[o, n], z_peer(at)))
-        pltpu.make_async_copy(src(z), dst, co_recv.at[o, n]).start()
+    def c_send_out(tensors, n, order):
+        def one(o, at):
+            src = c_out.at[o, n, c_rows(at)]
+            dst = outputs[o].at[:, pl.ds(n * col_step, col_step), lanes(half + z * HEAD_DIM)]
+
+            @pl.when(at != z)
+            def _():
+                send(src, dst, co_send.at[o, n], co_recv.at[o, n], z_peer(at))
+
+            @pl.when(at == z)
+            def _():
+                pltpu.make_async_copy(src, dst, co_recv.at[o, n]).start()
+
+        def step(i, carry):
+            for o in tensors:
+                one(o, order(i))
+            return carry
+
+        lax.fori_loop(0, RING, step, 0)
+
+    def round_from_here(i):
+        return lax.rem(z + i, RING)
+
+    def early_first(i):
+        later = RING // 2 + lax.rem(z + i // 2, RING // 2)
+        return jnp.where(lax.rem(i, 2) == 0, i // 2, later)
 
     def r_span(n):
         return pl.ds(n * row_step, row_step)
@@ -179,9 +207,10 @@
 
         @pl.when(x_lo == 0)
         def _():
+            for t in (KEY, VALUE):
+                spread(t, c_in.at[t, n])
             for t in (QUERY, GRAD):
                 take(c_in.at[t, n], ci_recv.at[t, n])
-            for t in range(4):
                 spread(t, c_in.at[t, n])
 
             def item(c, carry):
@@ -192,18 +221,20 @@
                     put(o, c, parts[o])
                 return carry
 
-            lax.fori_loop(0, col_step, item, 0, unroll=2)
+            lax.fori_loop(0, col_step, item, 0, unroll=4)
             c_out[DQUERY, n] = packed(n, DQUERY).astype(BF16)
-            c_send_out(DQUERY, n)
+            c_send_out((DQUERY,), n, round_from_here)
 
         @pl.when(x_lo == 1)
         def _():
-            for t in range(4):
+            for t in (KEY, VALUE):
                 take(c_in.at[t, n], ci_recv.at[t, n])
                 spread(t, c_in.at[t, n])
-            for t in (KEY, VALUE):
                 take(c_low.at[t, n], cl_recv.at[t, n])
                 spread(4 + t, c_low.at[t, n])
+            for t in (QUERY, GRAD):
+                take(c_in.at[t, n], ci_recv.at[t, n])
+                spread(t, c_in.at[t, n])
 
             def item(c, carry):
                 keys = jnp.concatenate([column(4 + KEY, c), column(KEY, c)], axis=0)
@@ -215,13 +246,14 @@
                     put(3 + o, c, parts[o][:col_len])
                 return carry
 
-            lax.fori_loop(0, col_step, item, 0, unroll=2)
+            lax.fori_loop(0, col_step, item, 0, unroll=4)
             for o in (DKEY, DVALUE):
                 c_part[o, n] = packed(n, 3 + o).astype(BF16)
                 send(c_part.at[o, n], c_back.at[o, n], cb_send.at[o, n], cb_recv.at[o, n], lo_peer)
             for o in (DQUERY, DKEY, DVALUE):
                 c_out[o, n] = packed(n, o).astype(BF16)
-                c_send_out(o, n)
+                last = n == 1 and o == DVALUE
+                c_send_out((o,), n, early_first if last else round_from_here)
 
     def c_finish(n):
         @pl.when(x_lo == 0)
@@ -229,7 +261,8 @@
             for o in (DKEY, DVALUE):
                 take(c_back.at[o, n], cb_recv.at[o, n])
                 c_out[o, n] = (packed(n, o) + c_back[o, n].astype(F32)).astype(BF16)
-                c_send_out(o, n)
+                last = n == 1 and o == DVALUE
+                c_send_out((o,), n, early_first if last else round_from_here)
 
     tile = row_len // 2
 
@@ -310,9 +343,22 @@
                 r_out[o, span] = (r_sum[o, span] + r_back[o, span].astype(F32)).astype(BF16)
                 r_send_out(o, n)
 
-    for n in range(2):
+    for n in range(COL_CHUNKS):
         for t in (KEY, VALUE, QUERY, GRAD):
             c_send_in(t, n)
+
+    @pl.when(z == 0)
+    def _():
+        signal_rings(ring_sem)
+        pl.semaphore_wait(ring_sem, RING + 1)
+        others(z, lambda at: signal(go_sem, z_peer(at)))
+
+    @pl.when(z != 0)
+    def _():
+        pl.semaphore_wait(go_sem, 1)
+
+    for n in range(ROW_CHUNKS):
+        for t in (KEY, VALUE, QUERY, GRAD):
             r_send_in(t, n)
 
     r_relay(0)
@@ -325,8 +371,8 @@
     r_finish(0)
     c_finish(0)
     c_work(1)
+    c_finish(1)
     r_finish(1)
-    c_finish(1)
 
     sent = (RING - 1) * row_count
     sent_cols = (RING - 1) * col_count
@@ -334,11 +380,6 @@
         for t in range(4):
             take(c_in.at[t, n, :sent], ci_send.at[t, n])
             take(r_in.at[t, r_span(n), :sent_cols], ri_send.at[t, n])
-        for o in range(3):
-            take(c_out.at[o, n, :sent], co_send.at[o, n])
-            take(r_out.at[o, r_span(n), :sent_cols], ro_send.at[o, n])
-            take(c_out.at[o, n], co_recv.at[o, n])
-            take(r_out.at[o, r_span(n)], ro_recv.at[o, n])
         for t in (KEY, VALUE):
             @pl.when(x_lo == 0)
             def _():
@@ -355,6 +396,13 @@
             @pl.when(x_hi == 1)
             def _():
                 take(r_part.at[t, r_span(n)], rb_send.at[t, n])
+        for o in (DQUERY, DKEY, DVALUE):
+            take(r_out.at[o, r_span(n), :sent_cols], ro_send.at[o, n])
+            take(r_out.at[o, r_span(n)], ro_recv.at[o, n])
+    for n in range(2):
+        for o in (DQUERY, DKEY, DVALUE):
+            take(c_out.at[o, n, :sent], co_send.at[o, n])
+            take(c_out.at[o, n], co_recv.at[o, n])
 
 
 def hand_out(*refs):
@@ -392,6 +440,7 @@
     for chunks in (COL_CHUNKS, ROW_CHUNKS):
         for arrays in (4, 2, 2, 3):
             scratch += [dma((arrays, chunks)), dma((arrays, chunks))]
+    scratch += [pltpu.SemaphoreType.REGULAR, pltpu.SemaphoreType.REGULAR]
     shape = jax.ShapeDtypeStruct(queries.shape, BF16)
     grads = pl.pallas_call(
         kernel,

time: 133 us -> 131 us (0.985); the launches traced: 132 us -> 129 us
  Pallas kernels: 132 us -> 128 us
    pallas_call x1, Pallas kernels: 130 us -> 126 us  [body(): pl.pallas_call(kernel, out_shape=(shape, shape, shape), in_specs=[pl.Bloc...]
where the time goes in v3:
time: 131 us; the launch traced here: 129 us
  Pallas kernels  128 us (98%)
    pallas_call x1, Pallas kernels, body(): pl.pallas_call(kernel, out_shape=(shape, shape, shape), in_specs=[pl.Bloc...  126 us

profile of v3, /device:TPU:4, one launch (start us, length us, event | category | flops | bytes accessed | tf_op | source)
XLA Modules:
  0.0 128.8 jit_solution(15840356793159693431)
XLA Ops:
  0.6 126.0 %shard_map.67 = (bf16[12,32,2048]{2,1,0:T(8,128)(2,1)S(1)}, bf16[12,32,2048]{2,1,0:T(8,128)(2,1)S(1)}, bf16[12,32,2048]{2,1,0:T(8,128)(2,1)S(1)}) custom-call(bf16[12,32,2048]{2,1,0:T(8,128)(2,1)} %q_ref.1, bf16[12,32,2048]{2,1,0:T(8,128)(2,1)} %k_ref.1, bf16[12,32,2048]{2,1,0:T(8,128)(2,1)} %v_ref.1, bf16[12,32,2048]{2,1,0:T(8,128)(2,1)} %g_ref.1), custom_call_target="tpu_custom_call" | custom-call | tf_op jit(solution)/shard_map/pallas_call | solution.py:445
  126.6 2.2 %shard_map.68 = (bf16[12,32,2048]{2,1,0:T(8,128)(2,1)}, bf16[12,32,2048]{2,1,0:T(8,128)(2,1)}, bf16[12,32,2048]{2,1,0:T(8,128)(2,1)}) custom-call(bf16[12,32,2048]{2,1,0:T(8,128)(2,1)S(1)} %get-tuple-element.6.refs_0_, bf16[12,32,2048]{2,1,0:T(8,128)(2,1)S(1)} %get-tuple-element.7.refs_1_, bf16[12,32,2048]{2,1,0:T(8,128)(2,1)S(1)} %get-tuple-element.8.refs_2_), custom_call_target="tpu_custom_call" | custom-call | tf_op jit(solution)/shard_map/pallas_call | solution.py:455

commit v4 on v3

--- a/solution.py
+++ b/solution.py
@@ -361,8 +361,8 @@
         for t in (KEY, VALUE, QUERY, GRAD):
             r_send_in(t, n)
 
+    c_relay(0)
     r_relay(0)
-    c_relay(0)
     r_work(0)
     r_relay(1)
     c_work(0)

time: 131 us -> 130 us (level); the launches traced: 129 us -> 130 us
  no operation moved by 1% of the time
where the time goes in v4:
time: 130 us
  Pallas kernels  129 us (99%)
    pallas_call x1, Pallas kernels, body(): pl.pallas_call(kernel, out_shape=(shape, shape, shape), in_specs=[pl.Bloc...  127 us

profile of v4, /device:TPU:4, one launch (start us, length us, event | category | flops | bytes accessed | tf_op | source)
XLA Modules:
  0.0 130.1 jit_solution(76253421102837080)
XLA Ops:
  0.6 127.2 %shard_map.67 = (bf16[12,32,2048]{2,1,0:T(8,128)(2,1)S(1)}, bf16[12,32,2048]{2,1,0:T(8,128)(2,1)S(1)}, bf16[12,32,2048]{2,1,0:T(8,128)(2,1)S(1)}) custom-call(bf16[12,32,2048]{2,1,0:T(8,128)(2,1)} %q_ref.1, bf16[12,32,2048]{2,1,0:T(8,128)(2,1)} %k_ref.1, bf16[12,32,2048]{2,1,0:T(8,128)(2,1)} %v_ref.1, bf16[12,32,2048]{2,1,0:T(8,128)(2,1)} %g_ref.1), custom_call_target="tpu_custom_call" | custom-call | tf_op jit(solution)/shard_map/pallas_call | solution.py:445
  127.9 2.2 %shard_map.68 = (bf16[12,32,2048]{2,1,0:T(8,128)(2,1)}, bf16[12,32,2048]{2,1,0:T(8,128)(2,1)}, bf16[12,32,2048]{2,1,0:T(8,128)(2,1)}) custom-call(bf16[12,32,2048]{2,1,0:T(8,128)(2,1)S(1)} %get-tuple-element.6.refs_0_, bf16[12,32,2048]{2,1,0:T(8,128)(2,1)S(1)} %get-tuple-element.7.refs_1_, bf16[12,32,2048]{2,1,0:T(8,128)(2,1)S(1)} %get-tuple-element.8.refs_2_), custom_call_target="tpu_custom_call" | custom-call | tf_op jit(solution)/shard_map/pallas_call | solution.py:455

commit v5 on v4

--- a/solution.py
+++ b/solution.py
@@ -193,10 +193,10 @@
                 )
 
     def spread(slot, ref):
-        f_in[slot] = ref[...].astype(F32).reshape(col_len * col_step, HEAD_DIM)
+        f_in[slot, : col_len * col_step] = ref[...].astype(F32).reshape(-1, HEAD_DIM)
 
     def packed(n, slot):
-        return f_out[n, slot].reshape(col_len, col_step, HEAD_DIM)
+        return f_out[n, slot, : col_len * col_step].reshape(col_len, col_step, HEAD_DIM)
 
     def c_work(n):
         def column(slot, c):
@@ -343,9 +343,8 @@
                 r_out[o, span] = (r_sum[o, span] + r_back[o, span].astype(F32)).astype(BF16)
                 r_send_out(o, n)
 
-    for n in range(COL_CHUNKS):
-        for t in (KEY, VALUE, QUERY, GRAD):
-            c_send_in(t, n)
+    for t in (KEY, VALUE, QUERY, GRAD):
+        c_send_in(t, 0)
 
     @pl.when(z == 0)
     def _():
@@ -357,9 +356,11 @@
     def _():
         pl.semaphore_wait(go_sem, 1)
 
-    for n in range(ROW_CHUNKS):
-        for t in (KEY, VALUE, QUERY, GRAD):
-            r_send_in(t, n)
+    for t in (KEY, VALUE, QUERY, GRAD):
+        r_send_in(t, 0)
+        c_send_in(t, 1)
+    for t in (KEY, VALUE, QUERY, GRAD):
+        r_send_in(t, 1)
 
     c_relay(0)
     r_relay(0)
@@ -420,7 +421,7 @@
     col_len, row_len = row_count * RING, col_count * RING
     c_shape = (COL_CHUNKS, col_len, col_step, HEAD_DIM)
     r_shape = (row_count, row_len, HEAD_DIM)
-    flat = (col_len * col_step, HEAD_DIM)
+    flat = (col_len * col_step + col_step, HEAD_DIM)
     dma = pltpu.SemaphoreType.DMA
     scratch = [
         pltpu.VMEM((4, *c_shape), BF16),

time: 130 us -> 130 us (level)
  no operation moved by 1% of the time
where the time goes in v5:
time: 130 us
  Pallas kernels  129 us (99%)
    pallas_call x1, Pallas kernels, body(): pl.pallas_call(kernel, out_shape=(shape, shape, shape), in_specs=[pl.Bloc...  127 us

profile of v5, /device:TPU:4, one launch (start us, length us, event | category | flops | bytes accessed | tf_op | source)
XLA Modules:
  0.0 130.0 jit_solution(2661978852896450985)
XLA Ops:
  0.6 127.2 %shard_map.67 = (bf16[12,32,2048]{2,1,0:T(8,128)(2,1)S(1)}, bf16[12,32,2048]{2,1,0:T(8,128)(2,1)S(1)}, bf16[12,32,2048]{2,1,0:T(8,128)(2,1)S(1)}) custom-call(bf16[12,32,2048]{2,1,0:T(8,128)(2,1)} %q_ref.1, bf16[12,32,2048]{2,1,0:T(8,128)(2,1)} %k_ref.1, bf16[12,32,2048]{2,1,0:T(8,128)(2,1)} %v_ref.1, bf16[12,32,2048]{2,1,0:T(8,128)(2,1)} %g_ref.1), custom_call_target="tpu_custom_call" | custom-call | tf_op jit(solution)/shard_map/pallas_call | solution.py:446
  127.8 2.2 %shard_map.68 = (bf16[12,32,2048]{2,1,0:T(8,128)(2,1)}, bf16[12,32,2048]{2,1,0:T(8,128)(2,1)}, bf16[12,32,2048]{2,1,0:T(8,128)(2,1)}) custom-call(bf16[12,32,2048]{2,1,0:T(8,128)(2,1)S(1)} %get-tuple-element.6.refs_0_, bf16[12,32,2048]{2,1,0:T(8,128)(2,1)S(1)} %get-tuple-element.7.refs_1_, bf16[12,32,2048]{2,1,0:T(8,128)(2,1)S(1)} %get-tuple-element.8.refs_2_), custom_call_target="tpu_custom_call" | custom-call | tf_op jit(solution)/shard_map/pallas_call | solution.py:456
